TPU v7x, 512 devices: a whole 4x4x16 slice. The times are simulated.
512 devices in a mesh: rows: 32 (over x, y, core), cols: 16 (over z).
Axes of the slice: x: 4, y: 4, z: 16, core: 2. Of those that a mesh axis runs over, the one named last changes fastest.
Arguments:
- images: bfloat16 [2, 3, 2048, 8192], P(None, None, 'rows', 'cols'), may hold values from -6 to 6
- enc_weight: bfloat16 [3, 8, 8, 128], replicated, may hold values from -0.4375 to 0.4375
- enc_bias: float32 [128], replicated, may hold values from -3 to 3
- mix_weight: bfloat16 [3, 3, 128, 128], replicated, may hold values from -0.1875 to 0.1875
- mix_bias: float32 [128], replicated, may hold values from -3 to 3
- agg_weight: bfloat16 [3, 3, 256, 128], replicated, may hold values from -0.125 to 0.125
- agg_bias: float32 [128], replicated, may hold values from -3 to 3
Outputs:
- aggregated: bfloat16 [512, 2048, 128], P(('rows', 'cols'))
All inputs are finite; a program needn't handle non-finite values.
Results may differ from a plain program's by a relative error of at most 0.0055.
Values may be sent and summed in bfloat16 or wider, within the bound.
A program may use at most 64 MiB of HBM per device.

v0:
```python
import math

import jax
import jax.numpy as jnp
from jax import lax
from jax.sharding import PartitionSpec as P

DISP = 256


def extended(x, sides, width):
    for axis, dim in sides:
        peers, length = (lax.axis_size(axis), x.shape[dim])
        up = [(i, (i + 1) % peers) for i in range(peers - 1)]
        down = [(j, i) for i, j in up]
        last = lax.slice_in_dim(x, length - width, length, axis=dim)
        initial = lax.slice_in_dim(x, 0, width, axis=dim)
        before = lax.ppermute(last, axis, up)
        after = lax.ppermute(initial, axis, down)
        x = jnp.concatenate([before, x, after], axis=dim)
    return x


def conv_three(padded, kernel):
    return lax.conv_general_dilated(
        padded,
        kernel,
        (1, 1),
        "VALID",
        dimension_numbers=("NHWC", "HWIO", "NHWC"),
        preferred_element_type=jnp.float32,
    )


def correlate(left, right_ext):
    rows_n, width, chans = left.shape
    block = DISP // 2
    count = width // block
    left_blocks = left.reshape(rows_n, count, block, chans)
    pieces = [
        right_ext[:, j * block : j * block + width].reshape(rows_n, count, block, chans)
        for j in range(DISP // block + 1)
    ]
    window = jnp.concatenate(pieces, axis=2)
    scores = jnp.einsum("rbic,rbjc->rbij", left_blocks, window, preferred_element_type=jnp.float32)
    scores = (scores * (1.0 / math.sqrt(chans))).astype(jnp.bfloat16)
    flat = scores.reshape(rows_n, count, block * (block + DISP))
    flat = jnp.pad(flat, ((0, 0), (0, 0), (0, block)))
    skew = flat.reshape(rows_n, count, block, block + DISP + 1)[..., 1 : DISP + 1]
    return jnp.flip(skew, axis=-1).reshape(rows_n, width, DISP)


def local(images, enc_weight, enc_bias, mix_weight, mix_bias, agg_weight, agg_bias):
    padded = extended(images, (("rows", 2), ("cols", 3)), 2)
    first = lax.conv_general_dilated(
        padded,
        enc_weight,
        (4, 4),
        "VALID",
        dimension_numbers=("NCHW", "IHWO", "NHWC"),
        preferred_element_type=jnp.float32,
    )
    lower = jnp.maximum(first + enc_bias, 0.0).astype(jnp.bfloat16)
    rimmed = extended(lower, (("rows", 1), ("cols", 2)), 1)
    feats = (lower.astype(jnp.float32) + conv_three(rimmed, mix_weight) + mix_bias).astype(
        jnp.bfloat16
    )
    moved = lax.all_to_all(feats, "cols", split_axis=1, concat_axis=2, tiled=True)
    right_ext = jnp.pad(moved[1], ((0, 0), (DISP, 0), (0, 0)))
    volume = correlate(moved[0], right_ext)
    edged = extended(volume, ((("rows", "cols"), 0),), 1)
    edged = jnp.pad(edged, ((0, 0), (1, 1), (0, 0)))
    return (conv_three(edged[None], agg_weight)[0] + agg_bias).astype(jnp.bfloat16)


def solution(mesh):
    return jax.shard_map(
        local,
        mesh=mesh,
        in_specs=(P(None, None, "rows", "cols"), P(), P(), P(), P(), P(), P()),
        out_specs=P(("rows", "cols"), None, None),
        check_vma=False,
    )
```

profile of v0, /device:TPU:6, one launch (start us, length us, event | category | flops | bytes accessed | tf_op | source)
XLA Modules:
  0.0 192.5 jit_solution(1474390578451437938)
XLA Ops:
  0.0 0.9 fusion.37
  0.9 1.9 collective-permute-start
  2.8 5.8 %collective-permute-start.1 = (bf16[2,3,2,512]{3,2,1,0:T(2,128)(2,1)S(1)}, bf16[2,3,2,512]{3,2,1,0:T(2,128)(2,1)S(1)}, u32[]{:S(2)}, u32[]{:S(2)}) collective-permute-start(bf16[2,3,2,512]{3,2,1,0:T(2,128)(2,1)S(1)} %get-tuple-element.16), channel_id=1, source_target_pairs={{16,0},{32,16},{48,32},{64,48},{80,64},{96,80},{112,96},{128,112},... | collective-permute-start | bytes 36872 | tf_op jit(solution)/shard_map/ppermute | solution.py:19
  8.6 1.4 collective-permute-done.1
  10.0 1.1 pad_maximum_fusion.2
  11.1 3.8 %collective-permute-start.2 = (bf16[2,3,68,2]{3,2,1,0:T(8,128)(2,1)S(1)}, bf16[2,3,68,2]{3,2,1,0:T(8,128)(2,1)S(1)}, u32[]{:S(2)}, u32[]{:S(2)}) collective-permute-start(bf16[2,3,68,2]{3,2,1,0:T(8,128)(2,1)S(1)} %get-tuple-element.13), channel_id=1, source_target_pairs={{0,1},{1,2},{2,3},{3,4},{4,5},{5,6},{6,7},{7,8},{8,9},{9,10},{10,1... | collective-permute-start | bytes 4904 | tf_op jit(solution)/shard_map/ppermute | solution.py:18
  14.9 1.3 collective-permute-start.3
  16.2 1.0 collective-permute-done.2
  17.2 4.3 %collective-permute-done.3 = bf16[2,3,68,2]{3,2,1,0:T(8,128)(2,1)S(1)} collective-permute-done((bf16[2,3,68,2]{3,2,1,0:T(8,128)(2,1)S(1)}, bf16[2,3,68,2]{3,2,1,0:T(8,128)(2,1)S(1)}, u32[]{:S(2)}, u32[]{:S(2)}) %collective-permute-start.3) | collective-permute-done | bytes 1664 | tf_op jit(solution)/shard_map/ppermute | solution.py:19
  21.6 1.5 maximum_bitcast_fusion.3
  23.1 0.1 pad.15.clone
  23.2 0.8 reshape.88
  24.0 0.2 slice.66
  24.2 0.6 copy_bitcast_fusion
  24.8 0.0 copy-start.3
  24.8 0.0 copy-start.4
  24.8 0.0 copy-start.7
  24.8 5.4 %copy.44 = bf16[3,68,16,75]{2,0,3,1:T(4,128)(2,1)} copy(bf16[3,68,16,75]{3,2,1,0:T(8,128)(2,1)S(1)} %copy_bitcast_fusion) | data formatting | bytes 979200 | tf_op jit(solution)/shard_map/conv_general_dilated | solution.py:55
  30.2 8.8 %maximum_convert_fusion = bf16[16,16,17,128]{3,1,2,0:T(8,128)(2,1)S(1)} fusion(bf16[3,68,16,75]{2,0,3,1:T(4,128)(2,1)} %copy.44, f32[128]{0:T(128)S(1)} %copy-done.4, pred[16,17]{0,1:T(8,128)(4,1)S(1)} %copy-done.7, bf16[3,8,8,128]{3,2,1,0:T(8,128)(2,1)S(1)} %copy-done.3), kind=kOutput, calls=%fused_computation.20 | convolution fusion | flops 216137728 | bytes 1653648 | tf_op jit(solution)/shard_map/conv_general_dilated | solution.py:55
  39.1 0.3 copy.47
  39.5 1.9 collective-permute-start.4
  41.5 0.1 copy.49
  41.6 5.8 %collective-permute-start.5 = (bf16[2,1,128,128]{3,1,2,0:T(2,128)(2,1)S(1)}, bf16[2,1,128,128]{3,1,2,0:T(2,128)(2,1)S(1)}, u32[]{:S(2)}, u32[]{:S(2)}) collective-permute-start(bf16[2,1,128,128]{3,1,2,0:T(2,128)(2,1)S(1)} %copy.49), channel_id=1, source_target_pairs={{16,0},{32,16},{48,32},{64,48},{80,64},{96,80},{112,96},{128,112},... | collective-permute-start | bytes 196616 | tf_op jit(solution)/shard_map/ppermute | solution.py:19
  47.4 0.2 slice_bitcast_fusion.2
  47.6 0.1 copy.50
  47.7 2.2 %collective-permute-done.5 = bf16[2,1,128,128]{3,1,2,0:T(2,128)(2,1)S(1)} collective-permute-done((bf16[2,1,128,128]{3,1,2,0:T(2,128)(2,1)S(1)}, bf16[2,1,128,128]{3,1,2,0:T(2,128)(2,1)S(1)}, u32[]{:S(2)}, u32[]{:S(2)}) %collective-permute-start.5) | collective-permute-done | bytes 65568 | tf_op jit(solution)/shard_map/ppermute | solution.py:19
  49.9 3.8 %collective-permute-start.6 = (bf16[2,18,1,128]{3,1,2,0:T(8,128)(2,1)S(1)}, bf16[2,18,1,128]{3,1,2,0:T(8,128)(2,1)S(1)}, u32[]{:S(2)}, u32[]{:S(2)}) collective-permute-start(bf16[2,18,1,128]{3,1,2,0:T(8,128)(2,1)S(1)} %get-tuple-element.5), channel_id=1, source_target_pairs={{0,1},{1,2},{2,3},{3,4},{4,5},{5,6},{6,7},{7,8},{8,9},{9,10},{10,1... | collective-permute-start | bytes 27656 | tf_op jit(solution)/shard_map/ppermute | solution.py:18
  53.7 1.5 collective-permute-start.7
  55.2 0.0 collective-permute-done.6
  55.2 5.1 %collective-permute-done.7 = bf16[2,18,1,128]{3,1,2,0:T(8,128)(2,1)S(1)} collective-permute-done((bf16[2,18,1,128]{3,1,2,0:T(8,128)(2,1)S(1)}, bf16[2,18,1,128]{3,1,2,0:T(8,128)(2,1)S(1)}, u32[]{:S(2)}, u32[]{:S(2)}) %collective-permute-start.7) | collective-permute-done | bytes 9248 | tf_op jit(solution)/shard_map/ppermute | solution.py:19
  60.3 0.9 maximum_bitcast_fusion
  61.2 0.9 copy.63
  62.2 0.0 copy-start.2
  62.2 0.0 copy-start.5
  62.2 0.9 pad.17.clone
  63.1 0.1 slice.72
  63.2 1.3 fusion.21
  64.6 2.8 %add_convert_fusion = bf16[16,16,17,128]{3,1,2,0:T(8,128)(2,1)S(1)} fusion(bf16[16,16,17,128]{3,1,2,0:T(8,128)(2,1)S(1)} %maximum_convert_fusion, bf16[3,3,128,128]{3,2,1,0:T(8,128)(2,1)S(1)} %copy-done.2, bf16[18,2,8,19,128]{4,1,3,2,0:T(2,128)(2,1)S(1)} %fusion.21, f32[128]{0:T(128)S(1)} %copy-done.5, pred[16,17]{0,1:T(8,128)(4,1)S(1)} %copy-done.7), kind=kOutput, calls=%fused_computation.19 | convolution fusion | flops 1286242304 | bytes 3924752 | tf_op jit(solution)/shard_map/conv_general_dilated | solution.py:25
  67.4 0.3 copy.53
  67.7 0.2 slice_bitcast_fusion.1
  67.8 0.3 copy.54
  68.1 61.4 %all_to_all.4 = bf16[2,16,128,128]{3,2,0,1:T(8,128)(2,1)S(1)} all-to-all(bf16[2,16,128,128]{3,2,0,1:T(8,128)(2,1)S(1)} %copy.54), channel_id=1, replica_groups=mesh['rows'=32,'cols'=16] {'cols'}, dimensions={1} | all-to-all | bytes 2097152 | tf_op jit(solution)/shard_map/all_to_all | solution.py:68
  129.5 0.1 fusion.36
  129.6 0.1 pad_slice_fusion.1
  129.7 0.8 multiply_convert_fusion
  130.5 1.7 reshape.83
  132.2 1.5 pad.13
  133.7 4.9 %reshape.84 = bf16[1,16,128,385]{3,2,1,0:T(8,128)(2,1)} reshape(bf16[1,16,49280]{2,1,0:T(8,128)(2,1)S(1)} %pad.13) | data formatting | bytes 3153920 | tf_op jit(solution)/shard_map/reshape | solution.py:49
  138.6 1.8 slice.76
  140.5 3.2 %rev.4 = bf16[1,16,128,256]{3,2,1,0:T(8,128)(2,1)S(1)} reverse(bf16[1,16,128,256]{3,2,1,0:T(8,128)(2,1)S(1)} %slice.76), dimensions={3} | reverse | bytes 2097152 | tf_op jit(solution)/shard_map/jit(_flip)/rev | solution.py:50
  143.7 8.5 %collective-permute-start.9 = (bf16[1,2048,256]{2,1,0:T(8,128)(2,1)S(1)}, bf16[1,2048,256]{2,1,0:T(8,128)(2,1)S(1)}, u32[]{:S(2)}, u32[]{:S(2)}) collective-permute-start(bf16[1,2048,256]{2,1,0:T(8,128)(2,1)S(1)} %bitcast.61), channel_id=1, source_target_pairs={{1,0},{2,1},{3,2},{4,3},{5,4},{6,5},{7,6},{8,7},{9,8},{10,9},{11,1... | collective-permute-start | bytes 3145736 | tf_op jit(solution)/shard_map/ppermute | solution.py:19
  152.2 2.1 %collective-permute-start.8 = (bf16[1,2048,256]{2,1,0:T(8,128)(2,1)S(1)}, bf16[1,2048,256]{2,1,0:T(8,128)(2,1)S(1)}, u32[]{:S(2)}, u32[]{:S(2)}) collective-permute-start(bf16[1,2048,256]{2,1,0:T(8,128)(2,1)S(1)} %bitcast.62), channel_id=1, source_target_pairs={{0,1},{1,2},{2,3},{3,4},{4,5},{5,6},{6,7},{7,8},{8,9},{9,10},{10,1... | collective-permute-start | bytes 3145736 | tf_op jit(solution)/shard_map/ppermute | solution.py:18
  154.3 17.6 %collective-permute-done.9 = bf16[1,2048,256]{2,1,0:T(8,128)(2,1)S(1)} collective-permute-done((bf16[1,2048,256]{2,1,0:T(8,128)(2,1)S(1)}, bf16[1,2048,256]{2,1,0:T(8,128)(2,1)S(1)}, u32[]{:S(2)}, u32[]{:S(2)}) %collective-permute-start.9) | collective-permute-done | bytes 1048608 | tf_op jit(solution)/shard_map/ppermute | solution.py:19
  171.9 5.9 %collective-permute-done.8 = bf16[1,2048,256]{2,1,0:T(8,128)(2,1)S(1)} collective-permute-done((bf16[1,2048,256]{2,1,0:T(8,128)(2,1)S(1)}, bf16[1,2048,256]{2,1,0:T(8,128)(2,1)S(1)}, u32[]{:S(2)}, u32[]{:S(2)}) %collective-permute-start.8) | collective-permute-done | bytes 1048608 | tf_op jit(solution)/shard_map/ppermute | solution.py:18
  177.8 1.1 fusion.14
  178.9 1.9 pad.19
  180.8 4.8 %reshape.104 = bf16[3,1,8,257,256]{4,3,2,0,1:T(8,128)(2,1)} reshape(bf16[3,1,2056,256]{3,2,0,1:T(8,128)(2,1)} %pad.19) | data formatting | bytes 6316032 | tf_op jit(solution)/shard_map/conv_general_dilated | solution.py:25
  185.6 2.5 %copy.58 = bf16[3,1,8,257,256]{4,2,3,0,1:T(8,128)(2,1)S(1)} copy(bf16[3,1,8,257,256]{4,3,2,0,1:T(8,128)(2,1)} %reshape.104) | data formatting | bytes 6316032 | tf_op jit(solution)/shard_map/conv_general_dilated | solution.py:25
  188.2 2.8 %fusion.24 = f32[1,8,257,128]{3,1,2,0:T(8,128)S(1)} fusion(bf16[3,3,256,128]{3,2,1,0:T(8,128)(2,1)S(1)} %copy-done, bf16[3,1,7,2,256]{4,2,3,0,1:T(8,128)(2,1)S(1)} %slice.77, bf16[3,1,8,257,256]{4,2,3,0,1:T(8,128)(2,1)S(1)} %copy.58, pred[8,257]{0,1:T(8,128)(4,1)S(1)} %copy-done.6), kind=kOutput, calls=%fused_computation.33 | convolution fusion | flops 1222489088 | bytes 4824072 | tf_op jit(solution)/shard_map/conv_general_dilated | solution.py:25
  191.0 0.0 copy-start.1
  191.0 0.2 copy.59
  191.2 0.1 reshape.108
  191.3 0.4 copy-done.1
  191.6 0.8 fusion.28
  (21 shorter events, 0.2 us)
Async XLA Ops:
  0.0 188.2 %copy-start = (bf16[3,3,256,128]{3,2,1,0:T(8,128)(2,1)S(1)}, bf16[3,3,256,128]{3,2,1,0:T(8,128)(2,1)}, u32[]{:S(2)}) copy-start(bf16[3,3,256,128]{3,2,1,0:T(8,128)(2,1)} %param.12) | copy-start | bytes 1769476
  0.9 7.7 %collective-permute-start = (bf16[2,3,2,512]{3,2,1,0:T(2,128)(2,1)S(1)}, bf16[2,3,2,512]{3,2,1,0:T(2,128)(2,1)S(1)}, u32[]{:S(2)}, u32[]{:S(2)}) collective-permute-start(bf16[2,3,2,512]{3,2,1,0:T(2,128)(2,1)S(1)} %get-tuple-element.15), channel_id=1, source_target_pairs={{0,16},{16,32},{32,48},{48,64},{64,80},{80,96},{96,112},{112,128},... | collective-permute-start | bytes 36872 | tf_op jit(solution)/shard_map/ppermute | solution.py:18
  2.8 7.1 %collective-permute-start.1 = (bf16[2,3,2,512]{3,2,1,0:T(2,128)(2,1)S(1)}, bf16[2,3,2,512]{3,2,1,0:T(2,128)(2,1)S(1)}, u32[]{:S(2)}, u32[]{:S(2)}) collective-permute-start(bf16[2,3,2,512]{3,2,1,0:T(2,128)(2,1)S(1)} %get-tuple-element.16), channel_id=1, source_target_pairs={{16,0},{32,16},{48,32},{64,48},{80,64},{96,80},{112,96},{128,112},... | collective-permute-start | bytes 36872 | tf_op jit(solution)/shard_map/ppermute | solution.py:19
  11.1 6.1 %collective-permute-start.2 = (bf16[2,3,68,2]{3,2,1,0:T(8,128)(2,1)S(1)}, bf16[2,3,68,2]{3,2,1,0:T(8,128)(2,1)S(1)}, u32[]{:S(2)}, u32[]{:S(2)}) collective-permute-start(bf16[2,3,68,2]{3,2,1,0:T(8,128)(2,1)S(1)} %get-tuple-element.13), channel_id=1, source_target_pairs={{0,1},{1,2},{2,3},{3,4},{4,5},{5,6},{6,7},{7,8},{8,9},{9,10},{10,1... | collective-permute-start | bytes 4904 | tf_op jit(solution)/shard_map/ppermute | solution.py:18
  14.9 6.6 %collective-permute-start.3 = (bf16[2,3,68,2]{3,2,1,0:T(8,128)(2,1)S(1)}, bf16[2,3,68,2]{3,2,1,0:T(8,128)(2,1)S(1)}, u32[]{:S(2)}, u32[]{:S(2)}) collective-permute-start(bf16[2,3,68,2]{3,2,1,0:T(8,128)(2,1)S(1)} %get-tuple-element.14), channel_id=1, source_target_pairs={{1,0},{2,1},{3,2},{4,3},{5,4},{6,5},{7,6},{8,7},{9,8},{10,9},{11,1... | collective-permute-start | bytes 4904 | tf_op jit(solution)/shard_map/ppermute | solution.py:19
  24.8 5.4 %copy-start.3 = (bf16[3,8,8,128]{3,2,1,0:T(8,128)(2,1)S(1)}, bf16[3,8,8,128]{3,2,1,0:T(8,128)(2,1)}, u32[]{:S(2)}) copy-start(bf16[3,8,8,128]{3,2,1,0:T(8,128)(2,1)} %param.8) | copy-start | bytes 147460
  24.8 5.4 %copy-start.4 = (f32[128]{0:T(128)S(1)}, f32[128]{0:T(128)}, u32[]{:S(2)}) copy-start(f32[128]{0:T(128)} %param.9) | copy-start | bytes 1540
  24.8 5.4 %copy-start.7 = (pred[16,17]{0,1:T(8,128)(4,1)S(1)}, pred[16,17]{0,1:T(8,128)(4,1)}, u32[]{:S(2)}) copy-start(pred[16,17]{0,1:T(8,128)(4,1)} %constant.26) | copy-start | bytes 820
  39.5 8.1 %collective-permute-start.4 = (bf16[2,1,128,128]{3,2,0,1:T(8,128)(2,1)S(1)}, bf16[2,1,128,128]{3,2,0,1:T(8,128)(2,1)S(1)}, u32[]{:S(2)}, u32[]{:S(2)}) collective-permute-start(bf16[2,1,128,128]{3,2,0,1:T(8,128)(2,1)S(1)} %slice_bitcast_fusion.6), channel_id=1, source_target_pairs={{0,16},{16,32},{32,48},{48,64},{64,80},{80,96},{96,112},{112,128},... | collective-permute-start | bytes 196616 | tf_op jit(solution)/shard_map/ppermute | solution.py:18
  41.6 8.3 %collective-permute-start.5 = (bf16[2,1,128,128]{3,1,2,0:T(2,128)(2,1)S(1)}, bf16[2,1,128,128]{3,1,2,0:T(2,128)(2,1)S(1)}, u32[]{:S(2)}, u32[]{:S(2)}) collective-permute-start(bf16[2,1,128,128]{3,1,2,0:T(2,128)(2,1)S(1)} %copy.49), channel_id=1, source_target_pairs={{16,0},{32,16},{48,32},{64,48},{80,64},{96,80},{112,96},{128,112},... | collective-permute-start | bytes 196616 | tf_op jit(solution)/shard_map/ppermute | solution.py:19
  49.9 5.3 %collective-permute-start.6 = (bf16[2,18,1,128]{3,1,2,0:T(8,128)(2,1)S(1)}, bf16[2,18,1,128]{3,1,2,0:T(8,128)(2,1)S(1)}, u32[]{:S(2)}, u32[]{:S(2)}) collective-permute-start(bf16[2,18,1,128]{3,1,2,0:T(8,128)(2,1)S(1)} %get-tuple-element.5), channel_id=1, source_target_pairs={{0,1},{1,2},{2,3},{3,4},{4,5},{5,6},{6,7},{7,8},{8,9},{9,10},{10,1... | collective-permute-start | bytes 27656 | tf_op jit(solution)/shard_map/ppermute | solution.py:18
  53.7 6.6 %collective-permute-start.7 = (bf16[2,18,1,128]{3,1,2,0:T(8,128)(2,1)S(1)}, bf16[2,18,1,128]{3,1,2,0:T(8,128)(2,1)S(1)}, u32[]{:S(2)}, u32[]{:S(2)}) collective-permute-start(bf16[2,18,1,128]{3,1,2,0:T(8,128)(2,1)S(1)} %get-tuple-element.6), channel_id=1, source_target_pairs={{1,0},{2,1},{3,2},{4,3},{5,4},{6,5},{7,6},{8,7},{9,8},{10,9},{11,1... | collective-permute-start | bytes 27656 | tf_op jit(solution)/shard_map/ppermute | solution.py:19
  62.2 2.4 %copy-start.2 = (bf16[3,3,128,128]{3,2,1,0:T(8,128)(2,1)S(1)}, bf16[3,3,128,128]{3,2,1,0:T(8,128)(2,1)}, u32[]{:S(2)}) copy-start(bf16[3,3,128,128]{3,2,1,0:T(8,128)(2,1)} %param.10) | copy-start | bytes 884740
  62.2 2.4 %copy-start.5 = (f32[128]{0:T(128)S(1)}, f32[128]{0:T(128)}, u32[]{:S(2)}) copy-start(f32[128]{0:T(128)} %param.11) | copy-start | bytes 1540
  143.7 28.2 %collective-permute-start.9 = (bf16[1,2048,256]{2,1,0:T(8,128)(2,1)S(1)}, bf16[1,2048,256]{2,1,0:T(8,128)(2,1)S(1)}, u32[]{:S(2)}, u32[]{:S(2)}) collective-permute-start(bf16[1,2048,256]{2,1,0:T(8,128)(2,1)S(1)} %bitcast.61), channel_id=1, source_target_pairs={{1,0},{2,1},{3,2},{4,3},{5,4},{6,5},{7,6},{8,7},{9,8},{10,9},{11,1... | collective-permute-start | bytes 3145736 | tf_op jit(solution)/shard_map/ppermute | solution.py:19
  152.2 25.6 %collective-permute-start.8 = (bf16[1,2048,256]{2,1,0:T(8,128)(2,1)S(1)}, bf16[1,2048,256]{2,1,0:T(8,128)(2,1)S(1)}, u32[]{:S(2)}, u32[]{:S(2)}) collective-permute-start(bf16[1,2048,256]{2,1,0:T(8,128)(2,1)S(1)} %bitcast.62), channel_id=1, source_target_pairs={{0,1},{1,2},{2,3},{3,4},{4,5},{5,6},{6,7},{7,8},{8,9},{9,10},{10,1... | collective-permute-start | bytes 3145736 | tf_op jit(solution)/shard_map/ppermute | solution.py:18
  185.6 2.6 %copy-start.6 = (pred[8,257]{0,1:T(8,128)(4,1)S(1)}, pred[8,257]{0,1:T(8,128)(4,1)}, u32[]{:S(2)}) copy-start(pred[8,257]{0,1:T(8,128)(4,1)} %constant.25) | copy-start | bytes 6172
  191.0 0.7 copy-start.1
where the time goes:
time: 193 us; the launch traced here: 192 us
  blocking collectives  61.4 us (32%)
  waiting for transfers between devices  37.4 us (19%)
  starting transfers between devices  36.4 us (19%)
  local copies, waits for them, and re-layouts  34.3 us (18%)
  matrix products  15.2 us (8%)
  other arithmetic  7.36 us (4%)
    all_to_all x1, blocking collectives, local(): lax.all_to_all(feats, 'cols', split_axis=1, concat_axis=2, tiled=True)  61.4 us
    ppermute x5, waiting for transfers between devices, extended(): after = lax.ppermute(initial, axis, down)  30.6 us
    ppermute x5, starting transfers between devices, extended(): after = lax.ppermute(initial, axis, down)  22.7 us
    ppermute x5, starting transfers between devices, extended(): before = lax.ppermute(last, axis, up)  13.6 us
    conv_general_dilated x1, matrix products, local(): lax.conv_general_dilated(padded, enc_weight, (4, 4), 'VALID', dimension_n...  8.84 us
    conv_general_dilated x6, local copies, waits for them, and re-layouts, conv_three(): lax.conv_general_dilated(padded, kernel, (1, 1), 'VALID', dimension_numbe...  7.77 us
    ppermute x5, waiting for transfers between devices, extended(): before = lax.ppermute(last, axis, up)  6.87 us
    conv_general_dilated x3, local copies, waits for them, and re-layouts, local(): lax.conv_general_dilated(padded, enc_weight, (4, 4), 'VALID', dimension_n...  6.42 us
  transfers between devices with their start and end apart: 10, of which 7 were waited for; matrix products, arithmetic and copies ran while one was open for 0% of the time, Pallas kernels for 0%

commit v1 on v0

v1 whole, which is shorter than its diff:
```python
import functools
import math

import jax
import jax.numpy as jnp
from jax import lax
from jax.experimental import pallas as pl
from jax.experimental.pallas import tpu as pltpu
from jax.sharding import PartitionSpec as P

DISP = 256
MESH = pl.DeviceIdType.MESH
BF = jnp.bfloat16
F32 = jnp.float32

TILE = 128
RIGHT = 144
ROWS = 544
LANES_L = 768
LANES = 2560


def dot(a, b):
    return lax.dot_general(a, b, (((1,), (0,)), ((), ())), preferred_element_type=F32)


def dot_t(a, b):
    return lax.dot_general(a, b, (((1,), (1,)), ((), ())), preferred_element_type=F32)


def iota(shape, dim):
    return lax.broadcasted_iota(jnp.int32, shape, dim)


def one_hot(cond):
    return jnp.where(cond, 1.0, 0.0).astype(BF)


def row_permutation():
    n, k = iota((256, 192), 0), iota((256, 192), 1)
    b = (n * 171) >> 11
    rest = n - 12 * b
    c, s = rest >> 2, rest & 3
    y = 4 * b - 10 + s
    return one_hot((y >= 0) & (y < 64) & (k == 64 * c + y))


def build_weights(enc_ref, mix_ref, agg_ref, wenc, wmix, wagg):
    row, col = iota((512, 192), 0), iota((512, 192), 1)
    n = row & 63
    j = 2 * (row >> 7) + ((row >> 6) & 1)
    b = (n * 43) >> 9
    rest = n - 12 * b
    base = 64 * (rest >> 2) + 8 * (rest & 3) + j
    for k in range(4):
        a = b - k
        good = (a >= 0) & (a <= 1) & (n < 60) & (col == base + 32 * a)
        part = dot(one_hot(good), enc_ref[...]).astype(BF)
        wenc[0, :, k * 128 : (k + 1) * 128] = part
        for jp in range(4):
            wenc[1, jp * 128 : jp * 128 + 64, k * 128 : (k + 1) * 128] = part[jp * 128 + 64 : jp * 128 + 128]
            wenc[1, jp * 128 + 64 : jp * 128 + 128, k * 128 : (k + 1) * 128] = part[jp * 128 : jp * 128 + 64]
    for beside in range(3):
        for out in range(2):
            lanes = slice((2 * beside + out) * 128, (2 * beside + out + 1) * 128)
            for a in range(4):
                if 0 <= a - out <= 2:
                    wmix[a * 128 : (a + 1) * 128, lanes] = mix_ref[a - out, beside]
                    wagg[a * 256 : (a + 1) * 256, lanes] = agg_ref[a - out, beside]
                else:
                    wmix[a * 128 : (a + 1) * 128, lanes] = jnp.zeros((128, 128), BF)
                    wagg[a * 256 : (a + 1) * 256, lanes] = jnp.zeros((256, 128), BF)


def build_selectors(sel):
    r, x = iota((512, 384), 0), iota((512, 384), 1)
    jj = r >> 6
    j = jnp.where(jj < 4, 2 * jj, 2 * jj - 7)
    q = r & 63
    sel[0] = one_hot(x == 90 + 4 * q + j)
    sel[1] = one_hot(x == 258 - 4 * q + j)


BLOCKS = (
    [(0, 64 * g, 64, 256 * g, 384, 0) for g in range(2)]
    + [(0, 128, 16, 512, 256, 0)]
    + [(1, RIGHT + 64 * g, 64, LANES_L + 1408 - 256 * g, 384, 0) for g in range(6)]
    + [(1, RIGHT + 384, 16, LANES_L, 256, 128)]
)


def gather_taps(even, odd, sel, store):
    for which, row, count, lane, width, skip in BLOCKS:
        lanes, cols = slice(lane, lane + width), slice(skip, skip + width)
        pick = sel[which, :, cols]
        if count != 64:
            pick = pick.reshape(8, 64, width)[:, :count].reshape(8 * count, width)
        half = 4 * count
        te = dot_t(pick[:half], even(lanes))
        to = dot_t(pick[half:], odd(lanes))
        for jp in range(4):
            store(slice(row, row + count), jp, te[jp * count : (jp + 1) * count], to[jp * count : (jp + 1) * count])


def compute_lower(u, wenc, kind, bias, valid, lower, first):
    acc = dot(u[...], wenc[kind])
    for k in range(4):
        part = jnp.maximum(acc[:, k * 128 : (k + 1) * 128] + bias, 0.0)
        lower[:, first + k * 128 : first + (k + 1) * 128] = jnp.where(valid, part, 0.0).astype(BF)


def kernel(
    img, enc_ref, encb_ref, mix_ref, mixb_ref, agg_ref, aggb_ref, out_ref,
    nat, perm, halo, edge, sel, wenc, wmix, wagg, u, lower, zs, feats, volume, stage,
    zsend, zrecv, rsend, rrecv, osend, orecv, own_sem,
):
    r, m = lax.axis_index("rows"), lax.axis_index("cols")
    nr, nz = lax.axis_size("rows"), lax.axis_size("cols")
    t = lax.rem(m + 1, nz)

    def zdev(d):
        return {"cols": lax.rem(m + d + nz, nz)}

    below, above = {"rows": lax.rem(r + 1, nr)}, {"rows": lax.rem(r + nr - 1, nr)}

    barrier = pltpu.get_barrier_semaphore()
    for d in range(1, 16):
        pl.semaphore_signal(barrier, inc=1, device_id=zdev(d), device_id_type=MESH)
    pl.semaphore_signal(barrier, inc=1, device_id=below, device_id_type=MESH)
    pl.semaphore_signal(barrier, inc=1, device_id=above, device_id_type=MESH)
    pl.semaphore_wait(barrier, 17)

    moves = [
        (img.at[1], slice(LANES_L + 1152, LANES_L + 1664), -1),
        (img.at[0], slice(128, 640), -1),
        (img.at[1], slice(LANES_L + 128, LANES_L + 640), 1),
        (img.at[0, :, 0:128], slice(640, 768), -2),
        (img.at[1, :, 0:128], slice(LANES_L + 1664, LANES_L + 1792), -2),
        (img.at[1, :, 384:512], slice(LANES_L, LANES_L + 128), 2),
    ]
    zcopies = [
        pltpu.make_async_remote_copy(
            src_ref=src, dst_ref=nat.at[:, lanes], send_sem=zsend.at[i], recv_sem=zrecv.at[i],
            device_id=zdev(d), device_id_type=MESH,
        )
        for i, (src, lanes, d) in enumerate(moves)
    ]
    for copy in zcopies:
        copy.start()

    build_weights(enc_ref, mix_ref, agg_ref, wenc, wmix, wagg)
    build_selectors(sel)
    shuffle = row_permutation()
    nat[:, 0:128] = img[0, :, 384:512]
    nat[:, LANES_L + 640 : LANES_L + 1152] = img[1]
    feats[RIGHT + 384 :, :] = jnp.zeros((128, 2304), BF)

    row128 = iota((ROWS, 128), 0)
    col_of = jnp.where(row128 < RIGHT, TILE * t - 9 + row128, TILE * t + 129 + RIGHT - row128)
    valid = (col_of >= 0) & (col_of < 2048)

    for copy in zcopies:
        copy.wait()

    def clear(lo, hi):
        nat[:, lo:hi] = jnp.zeros((192, hi - lo), BF)

    @pl.when(t == 0)
    def _():
        clear(0, 128)
        clear(LANES_L, LANES_L + 1152)

    @pl.when(t == 1)
    def _():
        clear(LANES_L, LANES_L + 640)

    @pl.when(t == 2)
    def _():
        clear(LANES_L, LANES_L + 128)

    @pl.when(t == nz - 1)
    def _():
        clear(640, 768)
        clear(LANES_L + 1664, LANES_L + 1792)

    for lo in range(0, LANES, 512):
        perm[:, lo : lo + 512] = dot(shuffle, nat[:, lo : lo + 512]).astype(BF)

    rcopies = [
        pltpu.make_async_remote_copy(
            src_ref=perm.at[lo : lo + 48], dst_ref=halo.at[i], send_sem=rsend.at[i], recv_sem=rrecv.at[i],
            device_id=to, device_id_type=MESH,
        )
        for i, (lo, to) in enumerate(((192, below), (16, above)))
    ]
    for copy in rcopies:
        copy.start()

    low = iota((1, 128), 1) < 64
    enc_bias = encb_ref[...]

    def store_mid(rows, jp, te, to):
        lanes = slice(jp * 128, (jp + 1) * 128)
        e, o = te[:, :128], to[:, :128]
        u[0, rows, lanes] = jnp.where(low, e, o).astype(BF)
        u[1, rows, lanes] = jnp.where(low, o, e).astype(BF)
        u[2, rows, lanes] = jnp.where(low, te[:, 128:], to[:, 128:]).astype(BF)

    def window(w):
        return slice(48 * w, 48 * w + 64)

    gather_taps(
        lambda lanes: jnp.concatenate([perm[window(w), lanes] for w in (1, 2, 3, 3)], axis=0),
        lambda lanes: jnp.concatenate([perm[window(w), lanes] for w in (2, 1, 3, 3)], axis=0),
        sel, store_mid,
    )
    compute_lower(u.at[0], wenc, 0, enc_bias, valid, lower, 512)
    compute_lower(u.at[1], wenc, 1, enc_bias, valid, lower, 1024)
    compute_lower(u.at[2], wenc, 0, enc_bias, valid, lower, 1536)

    for copy in rcopies:
        copy.wait()

    @pl.when(r == 0)
    def _():
        halo[0] = jnp.zeros((48, LANES), BF)

    @pl.when(r == nr - 1)
    def _():
        halo[1] = jnp.zeros((48, LANES), BF)

    edge[0:48] = perm[0:48] + halo[0]
    edge[48:64] = perm[48:64]
    edge[64:80] = perm[192:208]
    edge[80:128] = perm[208:256] + halo[1]

    def store_edge(rows, jp, te, to):
        lanes = slice(jp * 128, (jp + 1) * 128)
        u[0, rows, lanes] = jnp.where(low, te, to).astype(BF)
        u[1, rows, lanes] = jnp.where(low, to, te).astype(BF)

    gather_taps(
        lambda lanes: edge[:, lanes],
        lambda lanes: jnp.concatenate([edge[64:128, lanes], edge[0:64, lanes]], axis=0),
        sel, store_edge,
    )
    compute_lower(u.at[0], wenc, 0, enc_bias, valid, lower, 0)
    compute_lower(u.at[1], wenc, 1, enc_bias, valid, lower, 2048)

    @pl.when(r == 0)
    def _():
        lower[:, 0:256] = jnp.zeros((ROWS, 256), BF)

    @pl.when(r == nr - 1)
    def _():
        lower[:, 2304:2560] = jnp.zeros((ROWS, 256), BF)

    mix_bias = mixb_ref[...]
    rl = iota((RIGHT, 128), 0)
    ql = TILE * t - 8 + rl
    valid_l = (ql >= 0) & (ql < 2048)
    rr = iota((392, 128), 0)
    qr = TILE * t + 128 - rr
    valid_r = (qr >= 0) & (qr < 2048)

    def mix(s, carry):
        lanes = pl.ds(pl.multiple_of(s * 256, 256), 512)
        x = lower[:, lanes]
        z = dot(x, wmix[...])
        zs[:, 0:256] = z[:, 0:256]
        zs[:, 256:512] = z[:, 256:512] + x[:, 128:384].astype(F32)
        zs[:, 512:768] = z[:, 512:768]
        for k in range(2):
            a, b, c = (slice(i * 256 + k * 128, i * 256 + (k + 1) * 128) for i in range(3))
            dst = pl.ds(pl.multiple_of(s * 256 + k * 128, 128), 128)
            fl = zs[0:144, a] + zs[1:145, b] + zs[2:146, c] + mix_bias
            feats[0:144, dst] = jnp.where(valid_l, fl, 0.0).astype(BF)
            o = RIGHT
            fr = zs[o + 2 : o + 394, a] + zs[o + 1 : o + 393, b] + zs[o : o + 392, c] + mix_bias
            feats[o : o + 392, dst] = jnp.where(valid_r, fr, 0.0).astype(BF)
        return carry

    lax.fori_loop(0, 9, mix, 0)

    @pl.when(r == 0)
    def _():
        feats[0:RIGHT, 0:128] = jnp.zeros((RIGHT, 128), BF)

    @pl.when(r == nr - 1)
    def _():
        feats[0:RIGHT, 2176:2304] = jnp.zeros((RIGHT, 128), BF)

    def correlate(n, carry):
        lanes = pl.ds(pl.multiple_of(n * 128, 128), 128)
        scores = dot_t(feats[0:RIGHT, lanes], feats[RIGHT : RIGHT + 512, lanes])
        turned = jnp.concatenate(
            [
                pltpu.roll(scores[lo:hi], 376 + lo, 1, stride=1, stride_axis=0)[:, :DISP]
                for lo, hi in ((0, 64), (64, 128), (128, 144))
            ],
            axis=0,
        )
        dst = pl.ds(pl.multiple_of(n * DISP, DISP), DISP)
        volume[:, dst] = (turned * (1.0 / math.sqrt(128.0))).astype(BF)
        return carry

    lax.fori_loop(0, 18, correlate, 0)

    agg_bias = aggb_ref[...]
    place = pl.ds(pl.multiple_of(t * TILE, TILE), TILE)

    def send(p):
        return pltpu.make_async_remote_copy(
            src_ref=stage.at[p], dst_ref=out_ref.at[0, place], send_sem=osend.at[p], recv_sem=orecv.at[m],
            device_id={"cols": p}, device_id_type=MESH,
        )

    def aggregate(i, carry):
        s = lax.rem(i + lax.div(m, 2) + 1, 8)
        lanes = pl.ds(pl.multiple_of(s * 512, 512), 1024)
        z = dot(volume[:, lanes], wagg[...])
        zs[0:RIGHT] = z
        for k in range(2):
            a, b, c = (slice(i_ * 256 + k * 128, i_ * 256 + (k + 1) * 128) for i_ in range(3))
            stage[2 * s + k] = (zs[7:135, a] + zs[8:136, b] + zs[9:137, c] + agg_bias).astype(BF)
            p = 2 * s + k

            @pl.when(p != m)
            def _():
                send(p).start()

        return carry

    lax.fori_loop(0, 8, aggregate, 0)

    keep = pltpu.make_async_copy(stage.at[m], out_ref.at[0, place], own_sem)
    keep.start()
    keep.wait()

    def finish(p, carry):
        @pl.when(p != m)
        def _():
            send(p).wait_send()
            src = pl.ds(pl.multiple_of(lax.rem(p + 1, nz) * TILE, TILE), TILE)
            pltpu.make_async_remote_copy(
                src_ref=stage.at[p], dst_ref=out_ref.at[0, src], send_sem=osend.at[p], recv_sem=orecv.at[p],
                device_id={"cols": p}, device_id_type=MESH,
            ).wait_recv()

        return carry

    lax.fori_loop(0, 16, finish, 0)


def local(images, enc_weight, enc_bias, mix_weight, mix_bias, agg_weight, agg_bias):
    vmem = pl.BlockSpec(memory_space=pltpu.VMEM)
    return pl.pallas_call(
        kernel,
        out_shape=jax.ShapeDtypeStruct((1, 2048, 128), BF),
        in_specs=[vmem] * 7,
        out_specs=vmem,
        scratch_shapes=[
            pltpu.VMEM((192, LANES), BF),
            pltpu.VMEM((256, LANES), BF),
            pltpu.VMEM((2, 48, LANES), BF),
            pltpu.VMEM((128, LANES), BF),
            pltpu.VMEM((2, 512, 384), BF),
            pltpu.VMEM((2, 512, 512), BF),
            pltpu.VMEM((512, 768), BF),
            pltpu.VMEM((1024, 768), BF),
            pltpu.VMEM((3, ROWS, 512), BF),
            pltpu.VMEM((ROWS, 2560), BF),
            pltpu.VMEM((ROWS, 768), F32),
            pltpu.VMEM((RIGHT + 512, 2304), BF),
            pltpu.VMEM((RIGHT, 18 * DISP), BF),
            pltpu.VMEM((16, 128, 128), BF),
            pltpu.SemaphoreType.DMA((6,)),
            pltpu.SemaphoreType.DMA((6,)),
            pltpu.SemaphoreType.DMA((2,)),
            pltpu.SemaphoreType.DMA((2,)),
            pltpu.SemaphoreType.DMA((16,)),
            pltpu.SemaphoreType.DMA((16,)),
            pltpu.SemaphoreType.DMA,
        ],
        compiler_params=pltpu.CompilerParams(
            collective_id=0, has_side_effects=True, vmem_limit_bytes=48 * 1024 * 1024
        ),
        name="stereo",
    )(
        images.reshape(2, 192, 512),
        enc_weight.reshape(192, 128),
        enc_bias.reshape(1, 128),
        mix_weight,
        mix_bias.reshape(1, 128),
        agg_weight,
        agg_bias.reshape(1, 128),
    )


def solution(mesh):
    return jax.shard_map(
        local,
        mesh=mesh,
        in_specs=(P(None, None, "rows", "cols"), P(), P(), P(), P(), P(), P()),
        out_specs=P(("rows", "cols"), None, None),
        check_vma=False,
    )
```

time: 193 us -> 82.2 us (0.43)
  the two profiles are of different devices: /device:TPU:6 before, /device:TPU:1 now
where the time goes in v1:
time: 82.2 us; the launch traced here: 81.9 us
  Pallas kernels  76.6 us (93%)
  local copies, waits for them, and re-layouts  5.3 us (6%)
    pallas_call x1, Pallas kernels, local(): pl.pallas_call(kernel, out_shape=jax.ShapeDtypeStruct((1, 2048, 128), BF)...  76.6 us
    unnamed x15, local copies, waits for them, and re-layouts  5.3 us

profile of v1, /device:TPU:1, one launch (start us, length us, event | category | flops | bytes accessed | tf_op | source)
XLA Modules:
  0.0 81.9 jit_solution(11849168255270412195)
XLA Ops:
  0.0 0.0 copy-start.4
  0.0 0.0 copy-start.5
  0.0 0.0 copy-start.6
  0.0 0.6 copy-done.4
  0.7 0.0 copy-done.5
  0.7 0.0 copy-done.6
  0.7 0.0 copy-start
  0.7 1.1 %copy-done = bf16[3,3,256,128]{3,2,1,0:T(8,128)(2,1)S(1)} copy-done((bf16[3,3,256,128]{3,2,1,0:T(8,128)(2,1)S(1)}, bf16[3,3,256,128]{3,2,1,0:T(8,128)(2,1)}, u32[]{:S(2)}) %copy-start) | copy-done | bytes 589848
  1.8 0.0 copy-start.1
  1.8 1.0 %copy-done.1 = bf16[2,3,64,512]{3,2,1,0:T(8,128)(2,1)S(1)} copy-done((bf16[2,3,64,512]{3,2,1,0:T(8,128)(2,1)S(1)}, bf16[2,3,64,512]{3,2,1,0:T(8,128)(2,1)}, u32[]{:S(2)}) %copy-start.1) | copy-done | bytes 393240
  2.7 0.0 copy-start.2
  2.8 1.0 %copy-done.2 = bf16[3,3,128,128]{3,2,1,0:T(8,128)(2,1)S(1)} copy-done((bf16[3,3,128,128]{3,2,1,0:T(8,128)(2,1)S(1)}, bf16[3,3,128,128]{3,2,1,0:T(8,128)(2,1)}, u32[]{:S(2)}) %copy-start.2) | copy-done | bytes 294936
  3.7 0.0 copy-start.3
  3.7 0.8 copy-done.3
  4.5 76.6 %stereo.1 = bf16[1,2048,128]{2,1,0:T(8,128)(2,1)S(1)} custom-call(bf16[2,192,512]{2,1,0:T(8,128)(2,1)S(1)} %bitcast.5, bf16[192,128]{1,0:T(8,128)(2,1)S(1)} %bitcast.6, f32[1,128]{1,0:T(1,128)S(1)} %bitcast.7, bf16[3,3,128,128]{3,2,1,0:T(8,128)(2,1)S(1)} %copy-done.2, f32[1,128]{1,0:T(1,128)S(1)} %bitcast.8, bf16[3,3,256,128]{3,2,1,0:T(8,128)(2,1)S(1)} %copy-done, ...), custom_call_target="tpu_custom_call" | custom-call | tf_op jit(solution)/shard_map/stereo/pallas_call | solution.py:357
  81.1 0.8 copy.9
Async XLA Ops:
  0.0 0.7 copy-start.4
  0.0 0.7 copy-start.5
  0.0 0.7 copy-start.6
  0.7 1.1 %copy-start = (bf16[3,3,256,128]{3,2,1,0:T(8,128)(2,1)S(1)}, bf16[3,3,256,128]{3,2,1,0:T(8,128)(2,1)}, u32[]{:S(2)}) copy-start(bf16[3,3,256,128]{3,2,1,0:T(8,128)(2,1)} %agg_ref.1) | copy-start | bytes 1769476
  1.8 1.0 %copy-start.1 = (bf16[2,3,64,512]{3,2,1,0:T(8,128)(2,1)S(1)}, bf16[2,3,64,512]{3,2,1,0:T(8,128)(2,1)}, u32[]{:S(2)}) copy-start(bf16[2,3,64,512]{3,2,1,0:T(8,128)(2,1)} %param.7) | copy-start | bytes 1179652
  2.7 1.0 %copy-start.2 = (bf16[3,3,128,128]{3,2,1,0:T(8,128)(2,1)S(1)}, bf16[3,3,128,128]{3,2,1,0:T(8,128)(2,1)}, u32[]{:S(2)}) copy-start(bf16[3,3,128,128]{3,2,1,0:T(8,128)(2,1)} %mix_ref.1) | copy-start | bytes 884740
  3.7 0.8 copy-start.3

commit v2 on v1

v2 whole, which is shorter than its diff:
```python
import math

import jax
import jax.numpy as jnp
from jax import lax
from jax.experimental import pallas as pl
from jax.experimental.pallas import tpu as pltpu
from jax.sharding import PartitionSpec as P

DISP = 256
MESH = pl.DeviceIdType.MESH
BF = jnp.bfloat16
F32 = jnp.float32

TILE = 128
RIGHT = 144
ROWS = 544
LANES_L = 768
LANES = 2560


def dot(a, b):
    return lax.dot_general(a, b, (((1,), (0,)), ((), ())), preferred_element_type=F32)


def dot_t(a, b):
    return lax.dot_general(a, b, (((1,), (1,)), ((), ())), preferred_element_type=F32)


def iota(shape, dim):
    return lax.broadcasted_iota(jnp.int32, shape, dim)


def one_hot(cond):
    return jnp.where(cond, 1.0, 0.0).astype(BF)


def row_permutation():
    n, k = iota((64, 96), 0), iota((64, 96), 1)
    b = (n * 43) >> 9
    rest = n - 12 * b
    return one_hot((n < 60) & (k == 32 * (rest >> 2) + 4 * b + (rest & 3) + 6))


def build_weights(enc_ref, mix_ref, agg_ref, wenc, wmix, wagg):
    row, col = iota((512, 192), 0), iota((512, 192), 1)
    n = row & 63
    j = 2 * (row >> 7) + ((row >> 6) & 1)
    b = (n * 43) >> 9
    rest = n - 12 * b
    base = 64 * (rest >> 2) + 8 * (rest & 3) + j
    for k in range(4):
        a = b - k
        good = (a >= 0) & (a <= 1) & (n < 60) & (col == base + 32 * a)
        part = dot(one_hot(good), enc_ref[...]).astype(BF)
        wenc[0, :, k * 128 : (k + 1) * 128] = part
        for jp in range(4):
            wenc[1, jp * 128 : jp * 128 + 64, k * 128 : (k + 1) * 128] = part[jp * 128 + 64 : jp * 128 + 128]
            wenc[1, jp * 128 + 64 : jp * 128 + 128, k * 128 : (k + 1) * 128] = part[jp * 128 : jp * 128 + 64]
    for beside in range(3):
        for out in range(2):
            lanes = slice((2 * beside + out) * 128, (2 * beside + out + 1) * 128)
            for a in range(4):
                if 0 <= a - out <= 2:
                    wmix[a * 128 : (a + 1) * 128, lanes] = mix_ref[a - out, beside]
                    wagg[a * 256 : (a + 1) * 256, lanes] = agg_ref[a - out, beside]
                else:
                    wmix[a * 128 : (a + 1) * 128, lanes] = jnp.zeros((128, 128), BF)
                    wagg[a * 256 : (a + 1) * 256, lanes] = jnp.zeros((256, 128), BF)


def build_selectors(sel):
    r, x = iota((512, 384), 0), iota((512, 384), 1)
    jj = r >> 6
    j = jnp.where(jj < 4, 2 * jj, 2 * jj - 7)
    q = r & 63
    sel[0] = one_hot(x == 90 + 4 * q + j)
    sel[1] = one_hot(x == 258 - 4 * q + j)


BLOCKS = (
    [(0, 64 * g, 64, 256 * g, 384, 0) for g in range(2)]
    + [(0, 128, 16, 512, 256, 0)]
    + [(1, RIGHT + 64 * g, 64, LANES_L + 1408 - 256 * g, 384, 0) for g in range(6)]
    + [(1, RIGHT + 384, 16, LANES_L, 256, 128)]
)


def gather_taps(even, odd, sel, store):
    for which, row, count, lane, width, skip in BLOCKS:
        lanes, cols = slice(lane, lane + width), slice(skip, skip + width)
        pick = sel[which, :, cols]
        if count != 64:
            pick = pick.reshape(8, 64, width)[:, :count].reshape(8 * count, width)
        half = 4 * count
        te = dot_t(pick[:half], even(lanes))
        to = dot_t(pick[half:], odd(lanes))
        for jp in range(4):
            store(slice(row, row + count), jp, te[jp * count : (jp + 1) * count], to[jp * count : (jp + 1) * count])


def compute_lower(u, weights, bias, valid, lower, first):
    acc = dot(u[...], weights[...])
    for k in range(4):
        part = jnp.maximum(acc[:, k * 128 : (k + 1) * 128] + bias, 0.0)
        lanes = pl.ds(pl.multiple_of(first + k * 128, 128), 128)
        lower[:, lanes] = jnp.where(valid, part, 0.0).astype(BF)


def kernel(
    img, enc_hbm, encb_ref, mix_hbm, mixb_ref, agg_hbm, aggb_ref, out_ref,
    margin, enc_ref, mix_ref, agg_ref, nat, thin, strips, taken, sel, wenc, wmix, wagg,
    u, lower, zs, feats, volume, stage,
    in_sem, zsend, zrecv, rsend, rrecv, osend, orecv, own_sem, near_sem, far_sem,
):
    r, m = lax.axis_index("rows"), lax.axis_index("cols")
    nr, nz = lax.axis_size("rows"), lax.axis_size("cols")
    t = lax.rem(m + 1, nz)

    def zdev(d):
        return {"cols": lax.rem(m + d + nz, nz)}

    below, above = {"rows": lax.rem(r + 1, nr)}, {"rows": lax.rem(r + nr - 1, nr)}

    def signal(sem, device):
        pl.semaphore_signal(sem, inc=1, device_id=device, device_id_type=MESH)

    inner = slice(16, 80)
    ours = slice(LANES_L + 640, LANES_L + 1152)
    loads = [
        pltpu.make_async_copy(src, dst, in_sem.at[i])
        for i, (src, dst) in enumerate(
            (
                (img.at[0, :, :, 0:128], margin),
                (img.at[1], nat.at[:, inner, ours]),
                (img.at[0, :, :, 384:512], nat.at[:, inner, 0:128]),
                (enc_hbm, enc_ref),
                (mix_hbm, mix_ref),
                (agg_hbm, agg_ref),
            )
        )
    ]
    for load in loads:
        load.start()

    barrier = pltpu.get_barrier_semaphore()
    for device in (zdev(1), zdev(-1), zdev(2), zdev(-2), below, above):
        signal(barrier, device)
    pl.semaphore_wait(barrier, 6)

    def zcopy(i, src, dst, d):
        return pltpu.make_async_remote_copy(
            src_ref=src, dst_ref=dst, send_sem=zsend.at[i], recv_sem=zrecv.at[i],
            device_id=zdev(d), device_id_type=MESH,
        )

    moves = ((0, 128, -1), (1, LANES_L + 1152, -1), (1, LANES_L + 128, 1))

    def tiles(part, lo, hi):
        return [
            zcopy(3 * part + i, img.at[n, :, lo:hi], nat.at[:, 16 + lo : 16 + hi, lane : lane + 512], d)
            for i, (n, lane, d) in enumerate(moves)
        ]

    upper, rest = tiles(0, 0, 48), tiles(1, 48, 64)
    for copy in upper + rest:
        copy.start()
    signal(near_sem, zdev(2))
    signal(near_sem, zdev(-2))

    for load in loads[0:3]:
        load.wait()
    pick = iota((16, 128), 1) - iota((16, 128), 0)
    first, last = one_hot(pick == 0), one_hot(pick == 112)
    o = LANES_L + 640
    thin[0, :, 0:192] = dot_t(first, margin[...].reshape(192, 128)).astype(BF)
    thin[1, :, 0:192] = dot_t(first, nat[:, inner, o : o + 128].reshape(192, 128)).astype(BF)
    thin[2, :, 0:192] = dot_t(last, nat[:, inner, o + 384 : o + 512].reshape(192, 128)).astype(BF)
    edges = [
        zcopy(6, thin.at[0], strips.at[0, 0:16], -2),
        zcopy(7, thin.at[1], strips.at[1, 0:16], -2),
        zcopy(8, thin.at[2], strips.at[2, 112:128], 2),
    ]
    for copy in edges:
        copy.start()

    strips[0, 16:128] = jnp.zeros((112, 256), BF)
    strips[1, 16:128] = jnp.zeros((112, 256), BF)
    strips[2, 0:112] = jnp.zeros((112, 256), BF)
    build_selectors(sel)
    shuffle = row_permutation()
    for load in loads[3:]:
        load.wait()
    build_weights(enc_ref, mix_ref, agg_ref, wenc, wmix, wagg)
    feats[RIGHT + 384 :, :] = jnp.zeros((128, 2304), BF)

    row128 = iota((ROWS, 128), 0)
    col_of = jnp.where(row128 < RIGHT, TILE * t - 9 + row128, TILE * t + 129 + RIGHT - row128)
    valid = (col_of >= 0) & (col_of < 2048)

    def clear(rows, lo, hi):
        nat[:, rows, lo:hi] = jnp.zeros((3, rows.stop - rows.start, hi - lo), BF)

    pl.semaphore_wait(near_sem, 2)
    signal(far_sem, zdev(4))
    signal(far_sem, zdev(-4))

    for copy in edges:
        copy.wait()
    same = one_hot(iota((192, 192), 0) == iota((192, 192), 1))
    for i, lane in ((0, 640), (1, LANES_L + 1664), (2, LANES_L)):
        strip = dot_t(same, strips[i, :, 0:192]).astype(BF)
        nat[:, inner, lane : lane + 128] = strip.reshape(3, 64, 128)

    @pl.when(t == 0)
    def _():
        clear(inner, 0, 128)
        clear(inner, LANES_L, LANES_L + 128)
        clear(inner, LANES_L + 640, LANES_L + 1152)

    @pl.when((t == 1) | (t == 2))
    def _():
        clear(inner, LANES_L, LANES_L + 128)

    @pl.when(t == nz - 1)
    def _():
        clear(inner, 640, 768)
        clear(inner, LANES_L + 1664, LANES_L + 1792)

    def arrived(copies, rows):
        for copy in copies:
            copy.wait()

        @pl.when((t == 0) | (t == 1))
        def _():
            clear(rows, LANES_L + 128, LANES_L + 640)

    def rcopy(i, lo, to, device):
        return pltpu.make_async_remote_copy(
            src_ref=nat.at[:, lo : lo + 16], dst_ref=nat.at[:, to : to + 16], send_sem=rsend.at[i], recv_sem=rrecv.at[i],
            device_id=device, device_id_type=MESH,
        )

    up, down = rcopy(0, 16, 80, above), rcopy(1, 64, 0, below)

    arrived(upper, slice(16, 64))
    up.start()

    low = iota((1, 128), 1) < 64
    enc_bias = encb_ref[...]

    def take(w):
        for lo in range(0, LANES, 512):
            x = nat[:, 16 * w : 16 * w + 32, lo : lo + 512].reshape(96, 512)
            taken[w, :, lo : lo + 512] = dot(shuffle, x).astype(BF)

    def joined(order):
        return lambda lanes: jnp.concatenate([taken[w, :, lanes] for w in order], axis=0)

    def store_mid(rows, jp, te, to):
        lanes = slice(jp * 128, (jp + 1) * 128)
        u[1, rows, lanes] = jnp.where(low, te, to).astype(BF)
        u[2, rows, lanes] = jnp.where(low, to, te).astype(BF)

    def store_rest(rows, jp, te, to):
        lanes = slice(jp * 128, (jp + 1) * 128)
        e, o = te[:, :128], to[:, :128]
        u[0, rows, lanes] = jnp.where(low, e, o).astype(BF)
        u[3, rows, lanes] = jnp.where(low, o, e).astype(BF)
        u[4, rows, lanes] = jnp.where(low, te[:, 128:], to[:, 128:]).astype(BF)

    take(1)
    take(2)
    gather_taps(joined((1, 2)), joined((2, 1)), sel, store_mid)
    arrived(rest, slice(64, 80))
    down.start()
    pl.semaphore_wait(far_sem, 2)

    def gather_rest():
        up.wait()
        down.wait()

        @pl.when(r == 0)
        def _():
            clear(slice(0, 16), 0, LANES)

        @pl.when(r == nr - 1)
        def _():
            clear(slice(80, 96), 0, LANES)

        for w in (0, 3, 4):
            take(w)
        gather_taps(joined((0, 3, 4, 4)), joined((3, 0, 4, 4)), sel, store_rest)

    mix_bias = mixb_ref[...]
    ql = TILE * t - 8 + iota((RIGHT, 128), 0)
    valid_l = (ql >= 0) & (ql < 2048)
    qr = TILE * t + 128 - iota((392, 128), 0)
    valid_r = (qr >= 0) & (qr < 2048)

    def mix(s):
        lanes = pl.ds(pl.multiple_of(s * 256, 256), 512)
        x = lower[:, lanes]
        z = dot(x, wmix[...])
        zs[:, 0:256] = z[:, 0:256]
        zs[:, 256:512] = z[:, 256:512] + x[:, 128:384].astype(F32)
        zs[:, 512:768] = z[:, 512:768]
        for k in range(2):
            a, b, c = (slice(i * 256 + k * 128, i * 256 + (k + 1) * 128) for i in range(3))
            dst = pl.ds(pl.multiple_of(s * 256 + k * 128, 128), 128)
            fl = zs[0:144, a] + zs[1:145, b] + zs[2:146, c] + mix_bias
            feats[0:144, dst] = jnp.where(valid_l, fl, 0.0).astype(BF)
            o = RIGHT
            fr = zs[o + 2 : o + 394, a] + zs[o + 1 : o + 393, b] + zs[o : o + 392, c] + mix_bias
            feats[o : o + 392, dst] = jnp.where(valid_r, fr, 0.0).astype(BF)

        @pl.when((r == 0) & (s == 0))
        def _():
            feats[0:RIGHT, 0:128] = jnp.zeros((RIGHT, 128), BF)

        @pl.when((r == nr - 1) & (s == 8))
        def _():
            feats[0:RIGHT, 2176:2304] = jnp.zeros((RIGHT, 128), BF)

    def correlate(n):
        lanes = pl.ds(pl.multiple_of(n * 128, 128), 128)
        scores = dot_t(feats[0:RIGHT, lanes], feats[RIGHT : RIGHT + 512, lanes])
        turned = jnp.concatenate(
            [
                pltpu.roll(scores[lo:hi], 376 + lo, 1, stride=1, stride_axis=0)[:, :DISP]
                for lo, hi in ((0, 64), (64, 128), (128, 144))
            ],
            axis=0,
        )
        dst = pl.ds(pl.multiple_of(n * DISP, DISP), DISP)
        volume[:, dst] = (turned * (1.0 / math.sqrt(128.0))).astype(BF)

    agg_bias = aggb_ref[...]
    place = pl.ds(pl.multiple_of(t * TILE, TILE), TILE)

    def send(p):
        return pltpu.make_async_remote_copy(
            src_ref=stage.at[p], dst_ref=out_ref.at[0, place], send_sem=osend.at[p], recv_sem=orecv.at[m],
            device_id={"cols": p}, device_id_type=MESH,
        )

    def aggregate(s):
        lanes = pl.ds(pl.multiple_of(s * 512, 512), 1024)
        zs[0:RIGHT] = dot(volume[:, lanes], wagg[...])
        for k in range(2):
            a, b, c = (slice(i * 256 + k * 128, i * 256 + (k + 1) * 128) for i in range(3))
            p = 2 * s + k
            stage[p] = (zs[7:135, a] + zs[8:136, b] + zs[9:137, c] + agg_bias).astype(BF)

            @pl.when(p != m)
            def _():
                send(p).start()

    def step(i, carry):
        s = jnp.where(i < 5, 4 - i, i)

        @pl.when(i == 3)
        def _():
            gather_rest()

        @pl.when((i == 0) | (lax.rem(i, 2) == 1))
        def _():
            w = jnp.where(i == 0, 2, jnp.where(i < 5, lax.div(3 - i, 2), lax.div(i + 1, 2)))
            kind = jnp.where((w == 2) | (w == 3), 1, 0)
            compute_lower(u.at[w], wenc.at[kind], enc_bias, valid, lower, 512 * w)

            @pl.when((r == 0) & (w == 0))
            def _():
                lower[:, 0:256] = jnp.zeros((ROWS, 256), BF)

            @pl.when((r == nr - 1) & (w == 4))
            def _():
                lower[:, 2304:2560] = jnp.zeros((ROWS, 256), BF)

        mix(s)
        correlate(2 * s)
        correlate(2 * s + 1)

        @pl.when(i > 0)
        def _():
            aggregate(jnp.where(i < 5, s, s - 1))

        return carry

    lax.fori_loop(0, 9, step, 0)

    keep = pltpu.make_async_copy(stage.at[m], out_ref.at[0, place], own_sem)
    keep.start()
    keep.wait()

    def finish(p, carry):
        @pl.when(p != m)
        def _():
            send(p).wait_send()
            src = pl.ds(pl.multiple_of(lax.rem(p + 1, nz) * TILE, TILE), TILE)
            pltpu.make_async_remote_copy(
                src_ref=stage.at[p], dst_ref=out_ref.at[0, src], send_sem=osend.at[p], recv_sem=orecv.at[p],
                device_id={"cols": p}, device_id_type=MESH,
            ).wait_recv()

        return carry

    lax.fori_loop(0, 16, finish, 0)


def local(images, enc_weight, enc_bias, mix_weight, mix_bias, agg_weight, agg_bias):
    vmem, hbm = pl.BlockSpec(memory_space=pltpu.VMEM), pl.BlockSpec(memory_space=pltpu.HBM)
    return pl.pallas_call(
        kernel,
        out_shape=jax.ShapeDtypeStruct((1, 2048, 128), BF),
        in_specs=[hbm, hbm, vmem, hbm, vmem, hbm, vmem],
        out_specs=vmem,
        scratch_shapes=[
            pltpu.VMEM((3, 64, 128), BF),
            pltpu.VMEM((192, 128), BF),
            pltpu.VMEM((3, 3, 128, 128), BF),
            pltpu.VMEM((3, 3, 256, 128), BF),
            pltpu.VMEM((3, 96, LANES), BF),
            pltpu.VMEM((3, 16, 256), BF),
            pltpu.VMEM((3, 128, 256), BF),
            pltpu.VMEM((5, 64, LANES), BF),
            pltpu.VMEM((2, 512, 384), BF),
            pltpu.VMEM((2, 512, 512), BF),
            pltpu.VMEM((512, 768), BF),
            pltpu.VMEM((1024, 768), BF),
            pltpu.VMEM((5, ROWS, 512), BF),
            pltpu.VMEM((ROWS, 2560), BF),
            pltpu.VMEM((ROWS, 768), F32),
            pltpu.VMEM((RIGHT + 512, 2304), BF),
            pltpu.VMEM((RIGHT, 18 * DISP), BF),
            pltpu.VMEM((16, 128, 128), BF),
            pltpu.SemaphoreType.DMA((6,)),
            pltpu.SemaphoreType.DMA((9,)),
            pltpu.SemaphoreType.DMA((9,)),
            pltpu.SemaphoreType.DMA((2,)),
            pltpu.SemaphoreType.DMA((2,)),
            pltpu.SemaphoreType.DMA((16,)),
            pltpu.SemaphoreType.DMA((16,)),
            pltpu.SemaphoreType.DMA,
            pltpu.SemaphoreType.REGULAR,
            pltpu.SemaphoreType.REGULAR,
        ],
        compiler_params=pltpu.CompilerParams(
            collective_id=0, has_side_effects=True, vmem_limit_bytes=60 * 1024 * 1024
        ),
        name="stereo",
    )(
        images,
        enc_weight.reshape(192, 128),
        enc_bias.reshape(1, 128),
        mix_weight,
        mix_bias.reshape(1, 128),
        agg_weight,
        agg_bias.reshape(1, 128),
    )


def solution(mesh):
    return jax.shard_map(
        local,
        mesh=mesh,
        in_specs=(P(None, None, "rows", "cols"), P(), P(), P(), P(), P(), P()),
        out_specs=P(("rows", "cols"), None, None),
        check_vma=False,
    )
```

time: 82.2 us -> 61.1 us (0.74)
  the two profiles are of different devices: /device:TPU:1 before, /device:TPU:455 now
where the time goes in v2:
time: 61.1 us; the launch traced here: 60.9 us
  Pallas kernels  59.1 us (97%)
  local copies, waits for them, and re-layouts  1.87 us (3%)
    pallas_call x1, Pallas kernels, local(): pl.pallas_call(kernel, out_shape=jax.ShapeDtypeStruct((1, 2048, 128), BF)...  59.1 us
    unnamed x1, local copies, waits for them, and re-layouts  1.87 us

profile of v2, /device:TPU:455, one launch (start us, length us, event | category | flops | bytes accessed | tf_op | source)
XLA Modules:
  0.0 60.9 jit_solution(16422405925211886193)
XLA Ops:
  0.0 59.1 %stereo.1 = bf16[1,2048,128]{2,1,0:T(8,128)(2,1)} custom-call(bf16[2,3,64,512]{3,2,1,0:T(8,128)(2,1)} %img.1, bf16[192,128]{1,0:T(8,128)(2,1)} %bitcast.4, f32[1,128]{1,0:T(1,128)} %bitcast.5, bf16[3,3,128,128]{3,2,1,0:T(8,128)(2,1)} %mix_hbm.1, f32[1,128]{1,0:T(1,128)} %bitcast.6, bf16[3,3,256,128]{3,2,1,0:T(8,128)(2,1)} %agg_hbm.1, f32[1,128]{1,0:T(1,128)} %bitcast.7), custom_call_target="tpu_custom_call" | custom-call | tf_op jit(solution)/shard_map/stereo/pallas_call | solution.py:413
  59.1 1.9 %copy.9 = bf16[1,2048,128]{2,1,0:T(8,128)(2,1)} copy(bf16[1,2048,128]{2,1,0:T(8,128)(2,1)} %stereo.1) | data formatting | bytes 1048576

commit v3 on v2

--- a/solution.py
+++ b/solution.py
@@ -116,6 +116,9 @@
     r, m = lax.axis_index("rows"), lax.axis_index("cols")
     nr, nz = lax.axis_size("rows"), lax.axis_size("cols")
     t = lax.rem(m + 1, nz)
+    half = lax.div(nz, 2)
+    ahead = m < half
+    first_w, third_w = jnp.where(ahead, 3, 1), jnp.where(ahead, 1, 3)
 
     def zdev(d):
         return {"cols": lax.rem(m + d + nz, nz)}
@@ -156,14 +159,17 @@
 
     moves = ((0, 128, -1), (1, LANES_L + 1152, -1), (1, LANES_L + 128, 1))
 
-    def tiles(part, lo, hi):
-        return [
-            zcopy(3 * part + i, img.at[n, :, lo:hi], nat.at[:, 16 + lo : 16 + hi, lane : lane + 512], d)
-            for i, (n, lane, d) in enumerate(moves)
-        ]
-
-    upper, rest = tiles(0, 0, 48), tiles(1, 48, 64)
-    for copy in upper + rest:
+    def tiles(part, size, low_start, high_start):
+        copies = []
+        for i, (n, lane, d) in enumerate(moves):
+            target = lax.rem(m + d + nz, nz)
+            lo = pl.multiple_of(jnp.where(target < half, low_start, high_start), 16)
+            dst = nat.at[:, pl.ds(pl.multiple_of(lo + 16, 16), size), lane : lane + 512]
+            copies.append(zcopy(3 * part + i, img.at[n, :, pl.ds(lo, size)], dst, d))
+        return copies
+
+    middle, second, rest = tiles(0, 32, 16, 16), tiles(1, 16, 48, 0), tiles(2, 16, 0, 48)
+    for copy in middle:
         copy.start()
     signal(near_sem, zdev(2))
     signal(near_sem, zdev(-2))
@@ -177,11 +183,11 @@
     thin[1, :, 0:192] = dot_t(first, nat[:, inner, o : o + 128].reshape(192, 128)).astype(BF)
     thin[2, :, 0:192] = dot_t(last, nat[:, inner, o + 384 : o + 512].reshape(192, 128)).astype(BF)
     edges = [
-        zcopy(6, thin.at[0], strips.at[0, 0:16], -2),
-        zcopy(7, thin.at[1], strips.at[1, 0:16], -2),
-        zcopy(8, thin.at[2], strips.at[2, 112:128], 2),
+        zcopy(9, thin.at[0], strips.at[0, 0:16], -2),
+        zcopy(10, thin.at[1], strips.at[1, 0:16], -2),
+        zcopy(11, thin.at[2], strips.at[2, 112:128], 2),
     ]
-    for copy in edges:
+    for copy in edges + second + rest:
         copy.start()
 
     strips[0, 16:128] = jnp.zeros((112, 256), BF)
@@ -199,7 +205,8 @@
     valid = (col_of >= 0) & (col_of < 2048)
 
     def clear(rows, lo, hi):
-        nat[:, rows, lo:hi] = jnp.zeros((3, rows.stop - rows.start, hi - lo), BF)
+        size = rows.size if isinstance(rows, pl.Slice) else rows.stop - rows.start
+        nat[:, rows, lo:hi] = jnp.zeros((3, size, hi - lo), BF)
 
     pl.semaphore_wait(near_sem, 2)
     signal(far_sem, zdev(4))
@@ -235,50 +242,56 @@
         def _():
             clear(rows, LANES_L + 128, LANES_L + 640)
 
-    def rcopy(i, lo, to, device):
+    def rcopy(i, down):
+        lo, to = pl.multiple_of(jnp.where(down, 64, 16), 16), pl.multiple_of(jnp.where(down, 0, 80), 16)
         return pltpu.make_async_remote_copy(
-            src_ref=nat.at[:, lo : lo + 16], dst_ref=nat.at[:, to : to + 16], send_sem=rsend.at[i], recv_sem=rrecv.at[i],
-            device_id=device, device_id_type=MESH,
+            src_ref=nat.at[:, pl.ds(lo, 16)], dst_ref=nat.at[:, pl.ds(to, 16)], send_sem=rsend.at[i], recv_sem=rrecv.at[i],
+            device_id={"rows": lax.rem(r + jnp.where(down, 1, nr - 1), nr)}, device_id_type=MESH,
         )
 
-    up, down = rcopy(0, 16, 80, above), rcopy(1, 64, 0, below)
-
-    arrived(upper, slice(16, 64))
-    up.start()
+    halos = rcopy(0, ahead), rcopy(1, jnp.logical_not(ahead))
 
     low = iota((1, 128), 1) < 64
     enc_bias = encb_ref[...]
 
     def take(w):
         for lo in range(0, LANES, 512):
-            x = nat[:, 16 * w : 16 * w + 32, lo : lo + 512].reshape(96, 512)
+            x = nat[:, pl.ds(pl.multiple_of(16 * w, 16), 32), lo : lo + 512].reshape(96, 512)
             taken[w, :, lo : lo + 512] = dot(shuffle, x).astype(BF)
 
     def joined(order):
         return lambda lanes: jnp.concatenate([taken[w, :, lanes] for w in order], axis=0)
 
-    def store_mid(rows, jp, te, to):
-        lanes = slice(jp * 128, (jp + 1) * 128)
-        u[1, rows, lanes] = jnp.where(low, te, to).astype(BF)
-        u[2, rows, lanes] = jnp.where(low, to, te).astype(BF)
+    def gather_one(w):
+        def store_one(rows, jp, te, to):
+            u[w, rows, jp * 128 : (jp + 1) * 128] = jnp.where(low, te, to).astype(BF)
+
+        take(w)
+        gather_taps(joined((w, w)), joined((w, w)), sel, store_one)
 
     def store_rest(rows, jp, te, to):
         lanes = slice(jp * 128, (jp + 1) * 128)
         e, o = te[:, :128], to[:, :128]
         u[0, rows, lanes] = jnp.where(low, e, o).astype(BF)
-        u[3, rows, lanes] = jnp.where(low, o, e).astype(BF)
+        u[third_w, rows, lanes] = jnp.where(low, o, e).astype(BF)
         u[4, rows, lanes] = jnp.where(low, te[:, 128:], to[:, 128:]).astype(BF)
 
-    take(1)
-    take(2)
-    gather_taps(joined((1, 2)), joined((2, 1)), sel, store_mid)
-    arrived(rest, slice(64, 80))
-    down.start()
-    pl.semaphore_wait(far_sem, 2)
+    arrived(middle, slice(32, 64))
+
+    def gather_first():
+        gather_one(2)
+
+    def gather_second():
+        arrived(second, pl.ds(pl.multiple_of(jnp.where(ahead, 64, 16), 16), 16))
+        halos[0].start()
+        gather_one(first_w)
+        arrived(rest, pl.ds(pl.multiple_of(jnp.where(ahead, 16, 64), 16), 16))
+        halos[1].start()
+        pl.semaphore_wait(far_sem, 2)
 
     def gather_rest():
-        up.wait()
-        down.wait()
+        for copy in halos:
+            copy.wait()
 
         @pl.when(r == 0)
         def _():
@@ -288,9 +301,9 @@
         def _():
             clear(slice(80, 96), 0, LANES)
 
-        for w in (0, 3, 4):
+        for w in (0, third_w, 4):
             take(w)
-        gather_taps(joined((0, 3, 4, 4)), joined((3, 0, 4, 4)), sel, store_rest)
+        gather_taps(joined((0, third_w, 4, 4)), joined((third_w, 0, 4, 4)), sel, store_rest)
 
     mix_bias = mixb_ref[...]
     ql = TILE * t - 8 + iota((RIGHT, 128), 0)
@@ -357,16 +370,25 @@
                 send(p).start()
 
     def step(i, carry):
-        s = jnp.where(i < 5, 4 - i, i)
+        s = jnp.where(ahead, lax.rem(i + 4, 9), jnp.where(i < 5, 4 - i, i))
+
+        @pl.when(i == 0)
+        def _():
+            gather_first()
+
+        @pl.when(i == 1)
+        def _():
+            gather_second()
 
         @pl.when(i == 3)
         def _():
             gather_rest()
 
-        @pl.when((i == 0) | (lax.rem(i, 2) == 1))
-        def _():
-            w = jnp.where(i == 0, 2, jnp.where(i < 5, lax.div(3 - i, 2), lax.div(i + 1, 2)))
-            kind = jnp.where((w == 2) | (w == 3), 1, 0)
+        @pl.when((i == 0) | (i == 1) | (i == 3) | (i == 5) | (i == jnp.where(ahead, 6, 7)))
+        def _():
+            late = jnp.where(ahead, jnp.where(i == 3, 4, jnp.where(i == 5, 0, 1)), jnp.where(i == 3, 0, jnp.where(i == 5, 3, 4)))
+            w = jnp.where(i == 0, 2, jnp.where(i == 1, first_w, late))
+            kind = jnp.where(w == third_w, 1, 0)
             compute_lower(u.at[w], wenc.at[kind], enc_bias, valid, lower, 512 * w)
 
             @pl.when((r == 0) & (w == 0))
@@ -381,13 +403,19 @@
         correlate(2 * s)
         correlate(2 * s + 1)
 
-        @pl.when(i > 0)
-        def _():
-            aggregate(jnp.where(i < 5, s, s - 1))
+        below_s = ahead | (i > 4)
+
+        @pl.when((i > 0) & ((s > 0) | jnp.logical_not(below_s)))
+        def _():
+            aggregate(jnp.where(below_s, s - 1, s))
 
         return carry
 
     lax.fori_loop(0, 9, step, 0)
+
+    @pl.when(ahead)
+    def _():
+        aggregate(3)
 
     keep = pltpu.make_async_copy(stage.at[m], out_ref.at[0, place], own_sem)
     keep.start()
@@ -414,7 +442,7 @@
         kernel,
         out_shape=jax.ShapeDtypeStruct((1, 2048, 128), BF),
         in_specs=[hbm, hbm, vmem, hbm, vmem, hbm, vmem],
-        out_specs=vmem,
+        out_specs=hbm,
         scratch_shapes=[
             pltpu.VMEM((3, 64, 128), BF),
             pltpu.VMEM((192, 128), BF),
@@ -435,8 +463,8 @@
             pltpu.VMEM((RIGHT, 18 * DISP), BF),
             pltpu.VMEM((16, 128, 128), BF),
             pltpu.SemaphoreType.DMA((6,)),
-            pltpu.SemaphoreType.DMA((9,)),
-            pltpu.SemaphoreType.DMA((9,)),
+            pltpu.SemaphoreType.DMA((12,)),
+            pltpu.SemaphoreType.DMA((12,)),
             pltpu.SemaphoreType.DMA((2,)),
             pltpu.SemaphoreType.DMA((2,)),
             pltpu.SemaphoreType.DMA((16,)),

time: 61.1 us -> 60.1 us (0.984)
  the two profiles are of different devices: /device:TPU:455 before, /device:TPU:1 now
where the time goes in v3:
time: 60.1 us; the launch traced here: 59.9 us
  Pallas kernels  58 us (97%)
  local copies, waits for them, and re-layouts  1.87 us (3%)
    pallas_call x1, Pallas kernels, local(): pl.pallas_call(kernel, out_shape=jax.ShapeDtypeStruct((1, 2048, 128), BF)...  58 us
    unnamed x1, local copies, waits for them, and re-layouts  1.87 us

profile of v3, /device:TPU:1, one launch (start us, length us, event | category | flops | bytes accessed | tf_op | source)
XLA Modules:
  0.0 59.9 jit_solution(11872154489517111440)
XLA Ops:
  0.0 58.0 %stereo.1 = bf16[1,2048,128]{2,1,0:T(8,128)(2,1)} custom-call(bf16[2,3,64,512]{3,2,1,0:T(8,128)(2,1)} %img.1, bf16[192,128]{1,0:T(8,128)(2,1)} %bitcast.4, f32[1,128]{1,0:T(1,128)} %bitcast.5, bf16[3,3,128,128]{3,2,1,0:T(8,128)(2,1)} %mix_hbm.1, f32[1,128]{1,0:T(1,128)} %bitcast.6, bf16[3,3,256,128]{3,2,1,0:T(8,128)(2,1)} %agg_hbm.1, f32[1,128]{1,0:T(1,128)} %bitcast.7), custom_call_target="tpu_custom_call" | custom-call | tf_op jit(solution)/shard_map/stereo/pallas_call | solution.py:441
  58.0 1.9 %copy.9 = bf16[1,2048,128]{2,1,0:T(8,128)(2,1)} copy(bf16[1,2048,128]{2,1,0:T(8,128)(2,1)} %stereo.1) | data formatting | bytes 1048576

commit v4 on v3

--- a/solution.py
+++ b/solution.py
@@ -340,8 +340,8 @@
         scores = dot_t(feats[0:RIGHT, lanes], feats[RIGHT : RIGHT + 512, lanes])
         turned = jnp.concatenate(
             [
-                pltpu.roll(scores[lo:hi], 376 + lo, 1, stride=1, stride_axis=0)[:, :DISP]
-                for lo, hi in ((0, 64), (64, 128), (128, 144))
+                pltpu.roll(scores[lo:hi, :wide], (wide - 136 + lo) % wide, 1, stride=1, stride_axis=0)[:, :DISP]
+                for lo, hi, wide in ((0, 64, 512), (64, 128, 384), (128, 144, 384))
             ],
             axis=0,
         )

time: 60.1 us -> 60.1 us (level)
  no operation moved by 1% of the time
where the time goes in v4:
time: 60.1 us; the launch traced here: 59.9 us
  Pallas kernels  58 us (97%)
  local copies, waits for them, and re-layouts  1.87 us (3%)
    pallas_call x1, Pallas kernels, local(): pl.pallas_call(kernel, out_shape=jax.ShapeDtypeStruct((1, 2048, 128), BF)...  58 us
    unnamed x1, local copies, waits for them, and re-layouts  1.87 us

profile of v4, /device:TPU:1, one launch (start us, length us, event | category | flops | bytes accessed | tf_op | source)
XLA Modules:
  0.0 59.9 jit_solution(2031449434317764689)
XLA Ops:
  0.0 58.0 %stereo.1 = bf16[1,2048,128]{2,1,0:T(8,128)(2,1)} custom-call(bf16[2,3,64,512]{3,2,1,0:T(8,128)(2,1)} %img.1, bf16[192,128]{1,0:T(8,128)(2,1)} %bitcast.4, f32[1,128]{1,0:T(1,128)} %bitcast.5, bf16[3,3,128,128]{3,2,1,0:T(8,128)(2,1)} %mix_hbm.1, f32[1,128]{1,0:T(1,128)} %bitcast.6, bf16[3,3,256,128]{3,2,1,0:T(8,128)(2,1)} %agg_hbm.1, f32[1,128]{1,0:T(1,128)} %bitcast.7), custom_call_target="tpu_custom_call" | custom-call | tf_op jit(solution)/shard_map/stereo/pallas_call | solution.py:441
  58.0 1.9 %copy.9 = bf16[1,2048,128]{2,1,0:T(8,128)(2,1)} copy(bf16[1,2048,128]{2,1,0:T(8,128)(2,1)} %stereo.1) | data formatting | bytes 1048576
